TPU v7x, 256 devices: a whole 4x4x8 slice. The times are simulated.
256 devices in a mesh: row: 16 (over y, z_lo, core), col: 16 (over x, z_hi).
Axes of the slice: x: 4, y: 4, z: 8 (z_hi: 4, z_lo: 2; z = z_hi * 2 + z_lo), core: 2. Of those that a mesh axis runs over, the one named last changes fastest.
Arguments:
- query_single: bfloat16 [1024, 384], P('row'), may hold values from -6 to 6
- key_single: bfloat16 [4096, 384], P('col'), may hold values from -6 to 6
- query_weight: bfloat16 [384, 336], replicated, may hold values from -0.3125 to 0.3125
- key_weight: bfloat16 [384, 816], replicated, may hold values from -0.3125 to 0.3125
- pair_weight: bfloat16 [128, 12], replicated, may hold values from -1 to 1
- head_weight: float32 [12], replicated, may hold values from 0.2 to 2
- chain_bias: float32 [12], replicated, may hold values from -2 to 2
- pair: bfloat16 [1024, 4096, 128], P('row', 'col'), may hold values from -1000 to 1000
- residue_mask: int32 [4096], replicated, may hold values 0 or 1
- chain_index: int32 [4096], replicated, may hold values from 0 to 7, never falling along the last dimension, each value on 1 to 1024 neighbouring positions
- strip_offsets: int32 [16], replicated, may hold values from 0 to 4032, as said below
- grad_single_out: bfloat16 [1024, 192], P('row'), may hold values from -4 to 4
- grad_point_out: bfloat16 [1024, 288], P('row'), may hold values from -3 to 3
- grad_pair_out: bfloat16 [1024, 1536], P('row'), may hold values from -1 to 1
Outputs:
- grad_query_single: float32 [1024, 384], P('row')
- grad_key_single: float32 [4096, 384], P('col')
- grad_query_weight: float32 [384, 336], replicated
- grad_key_weight: float32 [384, 816], replicated
- grad_pair_weight: float32 [128, 12], replicated
- grad_pair: bfloat16 [1024, 4096, 128], P('row', 'col')
Inputs may be any that keep to these rules, and one draw needn't show every extreme that they name: `strip_offsets`: distinct multiples of 64; the first and the last strip of 64 residues are both among them.
All inputs are finite; a program needn't handle non-finite values.
Results may differ from a plain program's by a relative error of at most 0.012.
Values sent between devices are 32-bit elements; how exact they have to be, the bound alone decides.
No kernel may reach another device: no remote copies, remote signals or barrier semaphores. Data moves between devices by JAX's collectives and lax.ppermute only.
A program may use at most 64 MiB of HBM per device.

v0:
```python
import math
import jax
import jax.numpy as jnp
from jax import lax
from jax.sharding import PartitionSpec as P

H = 12
C = 16
P_SIZE = 4
PV = 8
DZ = 128
LOGIT_WEIGHT = math.sqrt(1.0 / 3.0)
MASKED_LOGIT = -100000.0


def local(
    query_single,
    key_single,
    query_weight,
    key_weight,
    pair_weight,
    head_weight,
    chain_bias,
    pair,
    residue_mask,
    chain_index,
    strip_offsets,
    grad_single_out,
    grad_point_out,
    grad_pair_out,
):
    query_rows = query_single.shape[0]
    key_rows = key_single.shape[0]
    head_cols = H * C
    point_cols = 3 * H * P_SIZE
    highest = lax.Precision.HIGHEST
    query_feats = jnp.dot(query_single, query_weight, preferred_element_type=jnp.float32).astype(
        jnp.bfloat16
    )
    key_feats = jnp.dot(key_single, key_weight, preferred_element_type=jnp.float32).astype(
        jnp.bfloat16
    )
    query_vec = query_feats[:, :head_cols].reshape(query_rows, H, C)
    query_pts = query_feats[:, head_cols:].reshape(query_rows, 3, H, P_SIZE)
    key_vec = key_feats[:, :head_cols].reshape(key_rows, H, C)
    value_vec = key_feats[:, head_cols : 2 * head_cols].reshape(key_rows, H, C)
    key_pts = key_feats[:, 2 * head_cols : 2 * head_cols + point_cols].reshape(
        key_rows, 3, H, P_SIZE
    )
    value_pts = key_feats[:, 2 * head_cols + point_cols :].reshape(key_rows, 3, H, PV)
    grad_vec = grad_single_out.reshape(query_rows, H, C)
    grad_pts = grad_point_out.reshape(query_rows, 3, H, PV)
    grad_pairs = grad_pair_out.reshape(query_rows, H, DZ)
    strip_begin = lax.dynamic_index_in_dim(strip_offsets, lax.axis_index("row"), 0, keepdims=False)
    key_begin = lax.axis_index("col") * key_rows
    query_live = lax.dynamic_slice_in_dim(residue_mask, strip_begin, query_rows, 0) == 1
    query_chain = lax.dynamic_slice_in_dim(chain_index, strip_begin, query_rows, 0)
    key_live = lax.dynamic_slice_in_dim(residue_mask, key_begin, key_rows, 0) == 1
    key_chain = lax.dynamic_slice_in_dim(chain_index, key_begin, key_rows, 0)
    live_pairs = query_live[:, None] & key_live[None, :]
    same_chain = (query_chain[:, None] == key_chain[None, :]).astype(jnp.float32)
    scalar = jnp.einsum("ihc,jhc->hij", query_vec, key_vec, preferred_element_type=jnp.float32)
    cross_term = jnp.einsum(
        "ixhp,jxhp->hij", query_pts, key_pts, preferred_element_type=jnp.float32
    )
    query_float = query_pts.astype(jnp.float32)
    key_float = key_pts.astype(jnp.float32)
    query_norm = jnp.sum(query_float * query_float, axis=(1, 3)).T
    key_norm = jnp.sum(key_float * key_float, axis=(1, 3)).T
    distance = query_norm[:, :, None] + key_norm[:, None, :] - 2.0 * cross_term
    pair_bias = jnp.einsum("ijc,ch->hij", pair, pair_weight, preferred_element_type=jnp.float32)
    point_coef = head_weight * (math.sqrt(2.0 / (9.0 * P_SIZE)) / 2.0)
    logits = LOGIT_WEIGHT * (
        scalar * C ** (-0.5) + pair_bias - point_coef[:, None, None] * distance
    )
    logits = logits + chain_bias[:, None, None] * same_chain[None]
    logits = jnp.where(live_pairs[None], logits, MASKED_LOGIT)
    row_top = lax.pmax(jnp.max(logits, axis=2), "col")
    upstream = jnp.einsum("ihc,jhc->hij", grad_vec, value_vec, preferred_element_type=jnp.float32)
    upstream = upstream + jnp.einsum(
        "ixhv,jxhv->hij", grad_pts, value_pts, preferred_element_type=jnp.float32
    )
    upstream = upstream + jnp.einsum(
        "ihc,ijc->hij", grad_pairs, pair, preferred_element_type=jnp.float32
    )
    exp_terms = jnp.exp(logits - row_top[:, :, None])
    row_total, moment = lax.psum(
        (jnp.sum(exp_terms, axis=2), jnp.sum(exp_terms * upstream, axis=2)), "col"
    )
    weights = exp_terms / row_total[:, :, None]
    centre = moment / row_total
    score_grad = jnp.where(live_pairs[None], weights * (upstream - centre[:, :, None]), 0.0)
    weight_bf = weights.astype(jnp.bfloat16)
    score_bf = score_grad.astype(jnp.bfloat16)
    scale_qk = LOGIT_WEIGHT * C ** (-0.5)
    grad_coef = -2.0 * LOGIT_WEIGHT * point_coef
    row_score = jnp.sum(score_bf, axis=2, dtype=jnp.float32)
    col_score = jnp.sum(score_bf, axis=1, dtype=jnp.float32)
    grad_qvec = scale_qk * jnp.einsum(
        "hij,jhc->ihc", score_bf, key_vec, preferred_element_type=jnp.float32
    )
    grad_qpts = grad_coef[None, None, :, None] * (
        query_float * row_score.T[:, None, :, None]
        - jnp.einsum("hij,jxhp->ixhp", score_bf, key_pts, preferred_element_type=jnp.float32)
    )
    query_part = jnp.concatenate(
        [grad_qvec.reshape(query_rows, -1), grad_qpts.reshape(query_rows, -1)], axis=1
    )
    query_grad = lax.psum(query_part, "col")
    grad_kvec = scale_qk * jnp.einsum(
        "hij,ihc->jhc", score_bf, query_vec, preferred_element_type=jnp.float32
    )
    grad_vvec = jnp.einsum("hij,ihc->jhc", weight_bf, grad_vec, preferred_element_type=jnp.float32)
    grad_kpts = grad_coef[None, None, :, None] * (
        key_float * col_score.T[:, None, :, None]
        - jnp.einsum("hij,ixhp->jxhp", score_bf, query_pts, preferred_element_type=jnp.float32)
    )
    grad_vpts = jnp.einsum(
        "hij,ixhv->jxhv", weight_bf, grad_pts, preferred_element_type=jnp.float32
    )
    key_part = jnp.concatenate(
        [
            grad_kvec.reshape(key_rows, -1),
            grad_vvec.reshape(key_rows, -1),
            grad_kpts.reshape(key_rows, -1),
            grad_vpts.reshape(key_rows, -1),
        ],
        axis=1,
    )
    bias_part = LOGIT_WEIGHT * jnp.einsum(
        "ijc,hij->ch", pair, score_bf, preferred_element_type=jnp.float32
    )
    key_weight_float = key_weight.astype(jnp.float32)
    key_single_float = key_single.astype(jnp.float32)
    key_grad = lax.psum(key_part, "row")
    grad_key_single = jnp.dot(key_grad, key_weight_float.T, precision=highest)
    grad_key_weight = lax.psum(jnp.dot(key_single_float.T, key_grad, precision=highest), "col")
    grad_pair_weight = lax.psum(bias_part, ("row", "col"))
    grad_query_single = jnp.dot(query_grad, query_weight.astype(jnp.float32).T, precision=highest)
    grad_query_weight = lax.psum(
        jnp.dot(query_single.astype(jnp.float32).T, query_grad, precision=highest), "row"
    )
    pair_grad = LOGIT_WEIGHT * jnp.einsum(
        "hij,ch->ijc", score_bf, pair_weight, preferred_element_type=jnp.float32
    )
    pair_grad = pair_grad + jnp.einsum(
        "hij,ihc->ijc", weight_bf, grad_pairs, preferred_element_type=jnp.float32
    )
    grad_pair = pair_grad.astype(jnp.bfloat16)
    return (
        grad_query_single,
        grad_key_single,
        grad_query_weight,
        grad_key_weight,
        grad_pair_weight,
        grad_pair,
    )


def solution(mesh):
    in_specs = (
        P("row", None),
        P("col", None),
        P(),
        P(),
        P(),
        P(),
        P(),
        P("row", "col", None),
        P(),
        P(),
        P(),
        P("row", None),
        P("row", None),
        P("row", None),
    )
    out_specs = (P("row", None), P("col", None), P(), P(), P(), P("row", "col", None))
    return jax.shard_map(local, mesh=mesh, in_specs=in_specs, out_specs=out_specs, check_vma=False)
```

profile of v0, /device:TPU:1, one launch (start us, length us, event | category | flops | bytes accessed | tf_op | source)
XLA Modules:
  0.0 589.7 jit_solution(5173191952428739225)
XLA Ops:
  7.2 1.3 dynamic_slice.16
  10.5 0.8 dynamic-slice_compare_fusion.1
  11.3 0.8 dynamic_slice.19
  12.0 0.8 dynamic_slice.20
  12.8 0.8 dynamic-slice_compare_fusion
  13.5 1.3 convolution_convert_fusion
  15.6 1.2 convolution_convert_fusion.1
  17.3 1.2 broadcast_multiply_fusion
  18.5 3.4 fusion.32
  23.4 41.9 %pmax.7 = f32[12,64]{1,0:T(8,128)S(1)} all-reduce(f32[12,64]{1,0:T(8,128)S(1)} %get-tuple-element.20), channel_id=1, replica_groups=mesh['row'=16,'col'=16] {'col'}, use_global_device_ids=true, to_apply=%region_3.4 | all-reduce | flops 768 | bytes 6144 | tf_op jit(solution)/shard_map/pmax | solution.py:78
  65.6 3.4 fusion.36
  70.0 2.5 fusion.17
  72.5 62.8 %all-reduce = (f32[12,64]{1,0:T(8,128)S(1)}, f32[12,64]{1,0:T(8,128)S(1)}) all-reduce(f32[12,64]{1,0:T(8,128)} %get-tuple-element.7, f32[12,64]{1,0:T(8,128)} %get-tuple-element.6), channel_id=1, replica_groups=mesh['row'=16,'col'=16] {'col'}, use_global_device_ids=true, to_apply=%region_7.8 | all-reduce | flops 1536 | bytes 12288 | tf_op jit(solution)/shard_map/psum | solution.py:87
  135.3 1.9 convert_reduce_fusion
  137.2 1.1 convolution_bitcast_fusion.4
  138.3 1.0 fusion.39
  139.3 1.0 convolution_multiply_fusion.1
  140.3 1.1 fusion.11
  141.5 1.0 pad_maximum_fusion
  143.7 134.9 %all-reduce.6.cloned.1.call-done = f32[256,816]{0,1:T(8,128)} async-done(((f32[256,816]{0,1:T(8,128)}), f32[256,816]{0,1:T(8,128)}) %all-reduce.6.cloned.1.call-update) | async-done | bytes 835600 | tf_op jit(solution)/shard_map/psum | solution.py:135
  278.6 3.0 convolution_bitcast_fusion
  281.7 1.3 fusion.18
  283.1 4.0 add_convert_fusion
  287.1 161.8 %all-reduce.10.cloned.1.call-done = (f32[64,336]{0,1:T(8,128)}, f32[384,816]{0,1:T(8,128)}) async-done(((f32[64,336]{0,1:T(8,128)}, f32[384,816]{0,1:T(8,128)}), (f32[64,336]{0,1:T(8,128)}, f32[384,816]{0,1:T(8,128)})) %all-reduce.10.cloned.1.call-update) | async-done | bytes 1339408 | tf_op jit(solution)/shard_map/psum | solution.py:109
  448.9 2.1 convolution_bitcast_fusion.3
  451.1 3.1 fusion.15
  454.2 82.8 %psum.55 = f32[128,12]{0,1:T(8,128)} all-reduce(f32[128,12]{0,1:T(8,128)S(1)} %fusion.15), channel_id=1, replica_groups=mesh['row'=16,'col'=16] {'row','col'}, use_global_device_ids=true, to_apply=%region_14.15 | all-reduce | flops 1536 | bytes 12288 | tf_op jit(solution)/shard_map/psum | solution.py:138
  537.0 1.8 fusion.38
  538.8 1.0 fusion.37
  539.8 40.5 %all-reduce.8.cloned.1.call-done = f32[384,336]{0,1:T(8,128)} async-done(((f32[384,336]{0,1:T(8,128)}), f32[384,336]{0,1:T(8,128)}) %all-reduce.8.cloned.1.call-update) | async-done | bytes 516112 | tf_op jit(solution)/shard_map/psum | solution.py:140
  580.3 1.9 copy.89
  582.2 1.0 copy.90
  (76 shorter events, 5.3 us)
Async XLA Ops:
  7.2 6.4 %copy-start = (bf16[384,816]{0,1:T(8,128)(2,1)S(1)}, bf16[384,816]{0,1:T(8,128)(2,1)}, u32[]{:S(2)}) copy-start(bf16[384,816]{0,1:T(8,128)(2,1)} %param.17) | copy-start | bytes 1880068
  7.2 271.4 %all-reduce.6.cloned.1.call-start = ((), (), s32[]{:S(2)}) async-start(), calls=%async_computation | async-start | bytes 1671168 | tf_op jit(solution)/shard_map/psum | solution.py:135
  14.9 7.7 %copy-start.2 = (bf16[256,816]{0,1:T(8,128)(2,1)}, bf16[256,816]{0,1:T(8,128)(2,1)S(1)}, u32[]{:S(2)}) copy-start(bf16[256,816]{0,1:T(8,128)(2,1)S(1)} %convolution_convert_fusion) | copy-start | bytes 1253380
  15.6 7.1 %copy-start.5 = (bf16[256,192]{0,1:T(8,128)(2,1)}, bf16[256,192]{0,1:T(8,128)(2,1)S(1)}, u32[]{:S(2)}) copy-start(bf16[256,192]{0,1:T(8,128)(2,1)S(1)} %get-tuple-element.16) | copy-start | bytes 294916
  15.6 7.1 %copy-start.21 = (f32[12]{0:T(128)S(1)}, f32[12]{0:T(128)}, u32[]{:S(2)}) copy-start(f32[12]{0:T(128)} %param.20) | copy-start | bytes 148
  17.0 6.3 %copy-start.12 = (bf16[64,192]{0,1:T(8,128)(2,1)}, bf16[64,192]{0,1:T(8,128)(2,1)S(1)}, u32[]{:S(2)}) copy-start(bf16[64,192]{0,1:T(8,128)(2,1)S(1)} %copy.40) | copy-start | bytes 73732
  17.1 6.3 %copy-start.9 = (bf16[256,3,12,4]{0,3,2,1:T(4,128)(2,1)}, bf16[256,3,12,4]{0,3,2,1:T(4,128)(2,1)S(1)}, u32[]{:S(2)}) copy-start(bf16[256,3,12,4]{0,3,2,1:T(4,128)(2,1)S(1)} %reshape.125) | copy-start | bytes 221188
  18.5 46.8 %copy-start.16 = (bf16[64,288]{1,0:T(8,128)(2,1)S(1)}, bf16[64,288]{1,0:T(8,128)(2,1)}, u32[]{:S(2)}) copy-start(bf16[64,288]{1,0:T(8,128)(2,1)} %param.26) | copy-start | bytes 110596
  18.5 46.9 %copy-start.13 = (bf16[64,1536]{1,0:T(8,128)(2,1)S(1)}, bf16[64,1536]{1,0:T(8,128)(2,1)}, u32[]{:S(2)}) copy-start(bf16[64,1536]{1,0:T(8,128)(2,1)} %param.27) | copy-start | bytes 589828
  22.7 42.7 %copy-start.15 = (pred[64,256]{1,0:T(8,128)(4,1)}, pred[64,256]{1,0:T(8,128)(4,1)S(1)}, u32[]{:S(2)}) copy-start(pred[64,256]{1,0:T(8,128)(4,1)S(1)} %get-tuple-element.24) | copy-start | bytes 49156
  22.7 46.2 %copy-start.17 = (bf16[64,192]{1,0:T(8,128)(2,1)S(1)}, bf16[64,192]{1,0:T(8,128)(2,1)}, u32[]{:S(2)}) copy-start(bf16[64,192]{1,0:T(8,128)(2,1)} %param.25) | copy-start | bytes 73732
  22.7 47.0 %slice-start = ((bf16[256,816]{0,1:T(8,128)(2,1)}), bf16[256,288]{0,1:T(8,128)(2,1)S(1)}, s32[]{:S(2)}) async-start(bf16[256,816]{0,1:T(8,128)(2,1)} %copy-done.2), calls=%async_computation.3 | async-start | bytes 294912 | tf_op jit(solution)/shard_map/slice | solution.py:50
  65.4 4.6 copy-start.11
  137.2 5.3 copy-start.10
  137.2 5.3 copy-start.19
  137.2 5.3 copy-start.20
  137.2 5.6 copy-start.6
  137.2 141.4 %copy-start.7 = (bf16[256,384]{1,0:T(8,128)(2,1)S(1)}, bf16[256,384]{1,0:T(8,128)(2,1)}, u32[]{:S(2)}) copy-start(bf16[256,384]{1,0:T(8,128)(2,1)} %param.15) | copy-start | bytes 589828
  141.4 140.3 %copy-start.18 = (bf16[128,12]{0,1:T(8,128)(2,1)S(1)}, bf16[128,12]{0,1:T(8,128)(2,1)}, u32[]{:S(2)}) copy-start(bf16[128,12]{0,1:T(8,128)(2,1)} %param.18) | copy-start | bytes 9220
  142.4 306.5 %all-reduce.10.cloned.1.call-start = ((), (), s32[]{:S(2)}) async-start(), calls=%async_computation.2 | async-start | bytes 2850816 | tf_op jit(solution)/shard_map/psum | solution.py:109
  281.7 298.6 %all-reduce.8.cloned.1.call-start = ((), (), s32[]{:S(2)}) async-start(), calls=%async_computation.1 | async-start | bytes 1032192 | tf_op jit(solution)/shard_map/psum | solution.py:140
  283.0 165.9 %copy-start.14 = (bf16[64,384]{1,0:T(8,128)(2,1)S(1)}, bf16[64,384]{1,0:T(8,128)(2,1)}, u32[]{:S(2)}) copy-start(bf16[64,384]{1,0:T(8,128)(2,1)} %param.14) | copy-start | bytes 147460
  287.1 249.9 %copy-start.1 = (f32[256,816]{0,1:T(8,128)S(1)}, f32[256,816]{0,1:T(8,128)}, u32[]{:S(2)}) copy-start(f32[256,816]{0,1:T(8,128)} %all-reduce.6.cloned.1.call-done) | copy-start | bytes 2506756
  287.1 251.7 %copy-start.4 = (bf16[384,336]{0,1:T(8,128)(2,1)S(1)}, bf16[384,336]{0,1:T(8,128)(2,1)}, u32[]{:S(2)}) copy-start(bf16[384,336]{0,1:T(8,128)(2,1)} %param.16) | copy-start | bytes 774148
  448.9 89.9 %copy-start.8 = (f32[64,336]{0,1:T(8,128)S(1)}, f32[64,336]{0,1:T(8,128)}, u32[]{:S(2)}) copy-start(f32[64,336]{0,1:T(8,128)} %get-tuple-element.12) | copy-start | bytes 258052
  451.1 131.1 %copy-start.3 = (f32[384,816]{0,1:T(8,128)S(1)}, f32[384,816]{0,1:T(8,128)}, u32[]{:S(2)}) copy-start(f32[384,816]{0,1:T(8,128)} %get-tuple-element.28) | copy-start | bytes 3760132
Sparse Core Ops, SparseCore 0:
  142.6 136.0 all-reduce.5
  282.1 166.7 all-reduce.9
  452.3 127.9 all-reduce.7
where the time goes:
time: 591 us; the launch traced here: 590 us
  waiting for transfers between devices  337 us (57%)
  blocking collectives  188 us (32%)
  matrix products  34.3 us (6%)
  between operations  16.1 us (3%)
  local copies, waits for them, and re-layouts  7.97 us (1%)
  other arithmetic  6.44 us (1%)
    psum x1, waiting for transfers between devices, local(): query_grad = lax.psum(query_part, 'col')  162 us
    psum x1, waiting for transfers between devices, local(): key_grad = lax.psum(key_part, 'row')  135 us
    psum x1, blocking collectives, local(): grad_pair_weight = lax.psum(bias_part, ('row', 'col'))  82.8 us
    psum x1, blocking collectives, local(): lax.psum((jnp.sum(exp_terms, axis=2), jnp.sum(exp_terms * upstream, axis=...  62.8 us
    pmax x1, blocking collectives, local(): row_top = lax.pmax(jnp.max(logits, axis=2), 'col')  41.9 us
    psum x1, waiting for transfers between devices, local(): lax.psum(jnp.dot(query_single.astype(jnp.float32).T, query_grad, precisio...  40.5 us
  transfers between devices with their start and end apart: 3, of which 3 were waited for; matrix products, arithmetic and copies ran while one was open for 2% of the time, Pallas kernels for 0%

commit v1 on v0

--- a/solution.py
+++ b/solution.py
@@ -3,6 +3,7 @@
 import jax.numpy as jnp
 from jax import lax
 from jax.sharding import PartitionSpec as P
+from jax.lax import all_gather
 
 H = 12
 C = 16
@@ -132,7 +133,7 @@
     )
     key_weight_float = key_weight.astype(jnp.float32)
     key_single_float = key_single.astype(jnp.float32)
-    key_grad = lax.psum(key_part, "row")
+    key_grad = jnp.sum(all_gather(key_part, "row"), axis=0)
     grad_key_single = jnp.dot(key_grad, key_weight_float.T, precision=highest)
     grad_key_weight = lax.psum(jnp.dot(key_single_float.T, key_grad, precision=highest), "col")
     grad_pair_weight = lax.psum(bias_part, ("row", "col"))

time: 591 us -> 567 us (0.959)
  waiting for transfers between devices: 337 us -> 292 us
  local copies, waits for them, and re-layouts: 7.97 us -> 23.6 us
  other arithmetic: 6.44 us -> 13.5 us
    psum x1 -> x0, waiting for transfers between devices: 135 us -> none  [local(): key_grad = lax.psum(key_part, 'row')]
    all_gather x0 -> x1, waiting for transfers between devices: none -> 92.6 us  [local(): key_grad = jnp.sum(all_gather(key_part, 'row'), axis=0)]
    unnamed x48 -> x43, local copies, waits for them, and re-layouts: 3.85 us -> 20.1 us
    reduce_sum x0 -> x1, other arithmetic: none -> 7.26 us  [local(): key_grad = jnp.sum(all_gather(key_part, 'row'), axis=0)]
where the time goes in v1:
time: 567 us; the launch traced here: 566 us
  waiting for transfers between devices  292 us (51%)
  blocking collectives  188 us (33%)
  matrix products  32.3 us (6%)
  local copies, waits for them, and re-layouts  23.6 us (4%)
  between operations  16.1 us (3%)
  other arithmetic  13.5 us (2%)
    psum x1, waiting for transfers between devices, local(): query_grad = lax.psum(query_part, 'col')  160 us
    all_gather x1, waiting for transfers between devices, local(): key_grad = jnp.sum(all_gather(key_part, 'row'), axis=0)  92.6 us
    psum x1, blocking collectives, local(): grad_pair_weight = lax.psum(bias_part, ('row', 'col'))  82.8 us
    psum x1, blocking collectives, local(): lax.psum((jnp.sum(exp_terms, axis=2), jnp.sum(exp_terms * upstream, axis=...  62.9 us
    pmax x1, blocking collectives, local(): row_top = lax.pmax(jnp.max(logits, axis=2), 'col')  42 us
    psum x1, waiting for transfers between devices, local(): lax.psum(jnp.dot(query_single.astype(jnp.float32).T, query_grad, precisio...  39.5 us
    unnamed x43, local copies, waits for them, and re-layouts  20.1 us
  transfers between devices with their start and end apart: 3, of which 3 were waited for; matrix products, arithmetic and copies ran while one was open for 2% of the time, Pallas kernels for 0%

profile of v1, /device:TPU:1, one launch (start us, length us, event | category | flops | bytes accessed | tf_op | source)
XLA Modules:
  0.0 565.9 jit_solution(8547526131472682496)
XLA Ops:
  7.2 1.3 dynamic_slice.16
  11.2 0.8 dynamic_slice.19
  12.8 0.8 dynamic-slice_compare_fusion.1
  13.6 1.2 convolution_convert_fusion.1
  14.8 1.3 convolution_convert_fusion
  16.7 1.2 broadcast_multiply_fusion
  17.8 3.4 fusion.31
  22.7 42.0 %pmax.7 = f32[12,64]{1,0:T(8,128)S(1)} all-reduce(f32[12,64]{1,0:T(8,128)S(1)} %get-tuple-element.20), channel_id=1, replica_groups=mesh['row'=16,'col'=16] {'col'}, use_global_device_ids=true, to_apply=%region_3.4 | all-reduce | flops 768 | bytes 6144 | tf_op jit(solution)/shard_map/pmax | solution.py:79
  64.9 3.4 fusion.35
  68.2 0.9 copy.66
  69.6 1.7 fusion.17
  71.4 62.9 %all-reduce = (f32[12,64]{1,0:T(8,128)S(1)}, f32[12,64]{1,0:T(8,128)S(1)}) all-reduce(f32[12,64]{1,0:T(8,128)S(1)} %get-tuple-element.7, f32[12,64]{1,0:T(8,128)S(1)} %get-tuple-element.6), channel_id=1, replica_groups=mesh['row'=16,'col'=16] {'col'}, use_global_device_ids=true, to_apply=%region_7.8 | all-reduce | flops 1536 | bytes 12288 | tf_op jit(solution)/shard_map/psum | solution.py:88
  134.4 1.7 convert_reduce_fusion
  136.1 1.1 convolution_bitcast_fusion.4
  137.1 1.0 fusion.38
  138.1 1.0 convolution_multiply_fusion.1
  139.4 1.0 pad_maximum_fusion
  141.7 92.6 %all-gather.3.cloned.1.call-done = f32[4096,816]{0,1:T(8,128)} async-done(((f32[256,816]{0,1:T(8,128)}), f32[4096,816]{0,1:T(8,128)}) %all-gather.3.cloned.1.call-update) | async-done | bytes 13369360 | tf_op jit(solution)/shard_map/all_gather | solution.py:136
  234.4 16.1 %copy.81 = f32[102,8,16,256]{3,2,1,0:T(8,128)} copy(f32[102,8,16,256]{3,1,2,0:T(8,128)} %bitcast.131) | data formatting | bytes 26738688
  250.5 7.3 %bitcast_reduce_fusion = f32[256,816]{0,1:T(8,128)S(1)} fusion(f32[102,8,16,256]{3,2,1,0:T(8,128)} %copy.81), kind=kLoop, calls=%fused_computation | loop fusion | flops 3133440 | bytes 14204928 | tf_op jit(solution)/shard_map/reduce_sum | solution.py:136
  257.7 1.9 convolution_bitcast_fusion
  259.9 1.3 fusion.18
  261.2 4.1 add_convert_fusion
  265.3 160.0 %all-reduce.7.cloned.1.call-done = (f32[64,336]{0,1:T(8,128)}, f32[384,816]{0,1:T(8,128)}) async-done(((f32[64,336]{0,1:T(8,128)}, f32[384,816]{0,1:T(8,128)}), (f32[64,336]{0,1:T(8,128)}, f32[384,816]{0,1:T(8,128)})) %all-reduce.7.cloned.1.call-update) | async-done | bytes 1339408 | tf_op jit(solution)/shard_map/psum | solution.py:110
  425.3 2.1 convolution_bitcast_fusion.3
  427.4 3.1 fusion.15
  430.5 82.8 %psum.47 = f32[128,12]{0,1:T(8,128)} all-reduce(f32[128,12]{0,1:T(8,128)S(1)} %fusion.15), channel_id=1, replica_groups=mesh['row'=16,'col'=16] {'row','col'}, use_global_device_ids=true, to_apply=%region_14.15 | all-reduce | flops 1536 | bytes 12288 | tf_op jit(solution)/shard_map/psum | solution.py:139
  513.3 1.8 fusion.37
  515.1 1.9 fusion.36
  517.0 39.5 %all-reduce.5.cloned.1.call-done = f32[384,336]{0,1:T(8,128)} async-done(((f32[384,336]{0,1:T(8,128)}), f32[384,336]{0,1:T(8,128)}) %all-reduce.5.cloned.1.call-update) | async-done | bytes 516112 | tf_op jit(solution)/shard_map/psum | solution.py:141
  556.5 1.9 copy.99
  558.3 1.0 copy.100
  (71 shorter events, 6.0 us)
Async XLA Ops:
  7.2 7.7 %copy-start = (bf16[384,816]{0,1:T(8,128)(2,1)S(1)}, bf16[384,816]{0,1:T(8,128)(2,1)}, u32[]{:S(2)}) copy-start(bf16[384,816]{0,1:T(8,128)(2,1)} %param.17) | copy-start | bytes 1880068
  7.2 227.2 %all-gather.3.cloned.1.call-start = ((), (), s32[]{:S(2)}) async-start(), calls=%async_computation.1 | async-start | bytes 14204928 | tf_op jit(solution)/shard_map/all_gather | solution.py:136
  16.2 6.5 %copy-start.1 = (bf16[256,816]{0,1:T(8,128)(2,1)}, bf16[256,816]{0,1:T(8,128)(2,1)S(1)}, u32[]{:S(2)}) copy-start(bf16[256,816]{0,1:T(8,128)(2,1)S(1)} %convolution_convert_fusion) | copy-start | bytes 1253380
  16.2 5.8 %copy-start.18 = (f32[12]{0:T(128)S(1)}, f32[12]{0:T(128)}, u32[]{:S(2)}) copy-start(f32[12]{0:T(128)} %param.20) | copy-start | bytes 148
  16.2 6.4 %copy-start.4 = (bf16[256,192]{0,1:T(8,128)(2,1)}, bf16[256,192]{0,1:T(8,128)(2,1)S(1)}, u32[]{:S(2)}) copy-start(bf16[256,192]{0,1:T(8,128)(2,1)S(1)} %get-tuple-element.16) | copy-start | bytes 294916
  16.4 6.3 %copy-start.10 = (bf16[64,192]{0,1:T(8,128)(2,1)}, bf16[64,192]{0,1:T(8,128)(2,1)S(1)}, u32[]{:S(2)}) copy-start(bf16[64,192]{0,1:T(8,128)(2,1)S(1)} %copy.61) | copy-start | bytes 73732
  16.5 6.2 %copy-start.7 = (bf16[256,3,12,4]{0,3,2,1:T(4,128)(2,1)}, bf16[256,3,12,4]{0,3,2,1:T(4,128)(2,1)S(1)}, u32[]{:S(2)}) copy-start(bf16[256,3,12,4]{0,3,2,1:T(4,128)(2,1)S(1)} %reshape.125) | copy-start | bytes 221188
  17.8 46.9 %copy-start.12 = (bf16[64,1536]{1,0:T(8,128)(2,1)S(1)}, bf16[64,1536]{1,0:T(8,128)(2,1)}, u32[]{:S(2)}) copy-start(bf16[64,1536]{1,0:T(8,128)(2,1)} %param.27) | copy-start | bytes 589828
  22.0 46.3 %copy-start.14 = (pred[64,256]{1,0:T(8,128)(4,1)}, pred[64,256]{1,0:T(8,128)(4,1)S(1)}, u32[]{:S(2)}) copy-start(pred[64,256]{1,0:T(8,128)(4,1)S(1)} %get-tuple-element.24) | copy-start | bytes 49156
  22.0 47.2 %copy-start.15 = (bf16[64,192]{1,0:T(8,128)(2,1)S(1)}, bf16[64,192]{1,0:T(8,128)(2,1)}, u32[]{:S(2)}) copy-start(bf16[64,192]{1,0:T(8,128)(2,1)} %param.25) | copy-start | bytes 73732
  22.7 46.6 %slice-start = ((bf16[256,816]{0,1:T(8,128)(2,1)}), bf16[256,288]{0,1:T(8,128)(2,1)S(1)}, s32[]{:S(2)}) async-start(bf16[256,816]{0,1:T(8,128)(2,1)} %copy-done.1), calls=%async_computation.3 | async-start | bytes 294912 | tf_op jit(solution)/shard_map/slice | solution.py:51
  69.2 65.1 %copy-start.9 = (bf16[64,288]{0,1:T(8,128)(2,1)}, bf16[64,288]{0,1:T(8,128)(2,1)S(1)}, u32[]{:S(2)}) copy-start(bf16[64,288]{0,1:T(8,128)(2,1)S(1)} %copy.66) | copy-start | bytes 110596
  69.3 65.0 %copy-start.11 = (bf16[64,192]{0,1:T(8,128)(2,1)}, bf16[64,192]{0,1:T(8,128)(2,1)S(1)}, u32[]{:S(2)}) copy-start(bf16[64,192]{0,1:T(8,128)(2,1)S(1)} %copy.65) | copy-start | bytes 73732
  71.4 67.7 %copy-start.8 = (bf16[256,3,12,4]{0,3,2,1:T(4,128)(2,1)S(1)}, bf16[256,3,12,4]{0,3,2,1:T(4,128)(2,1)}, u32[]{:S(2)}) copy-start(bf16[256,3,12,4]{0,3,2,1:T(4,128)(2,1)} %copy-done.7) | copy-start | bytes 221188
  71.4 67.7 %copy-start.17 = (f32[12]{0:T(128)S(1)}, f32[12]{0:T(128)}, u32[]{:S(2)}) copy-start(f32[12]{0:T(128)} %get-tuple-element.18) | copy-start | bytes 148
  134.3 6.5 %copy-start.5 = (bf16[256,192]{0,1:T(8,128)(2,1)S(1)}, bf16[256,192]{0,1:T(8,128)(2,1)}, u32[]{:S(2)}) copy-start(bf16[256,192]{0,1:T(8,128)(2,1)} %copy-done.4) | copy-start | bytes 294916
  140.4 284.9 %all-reduce.7.cloned.1.call-start = ((), (), s32[]{:S(2)}) async-start(), calls=%async_computation.2 | async-start | bytes 2850816 | tf_op jit(solution)/shard_map/psum | solution.py:110
  250.5 7.3 %copy-start.6 = (bf16[256,384]{1,0:T(8,128)(2,1)S(1)}, bf16[256,384]{1,0:T(8,128)(2,1)}, u32[]{:S(2)}) copy-start(bf16[256,384]{1,0:T(8,128)(2,1)} %param.15) | copy-start | bytes 589828
  250.5 9.4 %copy-start.16 = (bf16[128,12]{0,1:T(8,128)(2,1)S(1)}, bf16[128,12]{0,1:T(8,128)(2,1)}, u32[]{:S(2)}) copy-start(bf16[128,12]{0,1:T(8,128)(2,1)} %param.18) | copy-start | bytes 9220
  259.6 296.9 %all-reduce.5.cloned.1.call-start = ((), (), s32[]{:S(2)}) async-start(), calls=%async_computation | async-start | bytes 1032192 | tf_op jit(solution)/shard_map/psum | solution.py:141
  261.2 164.1 %copy-start.13 = (bf16[64,384]{1,0:T(8,128)(2,1)S(1)}, bf16[64,384]{1,0:T(8,128)(2,1)}, u32[]{:S(2)}) copy-start(bf16[64,384]{1,0:T(8,128)(2,1)} %param.14) | copy-start | bytes 147460
  265.3 249.8 %copy-start.3 = (bf16[384,336]{0,1:T(8,128)(2,1)S(1)}, bf16[384,336]{0,1:T(8,128)(2,1)}, u32[]{:S(2)}) copy-start(bf16[384,336]{0,1:T(8,128)(2,1)} %param.16) | copy-start | bytes 774148
  427.4 131.0 %copy-start.2 = (f32[384,816]{0,1:T(8,128)S(1)}, f32[384,816]{0,1:T(8,128)}, u32[]{:S(2)}) copy-start(f32[384,816]{0,1:T(8,128)} %get-tuple-element.28) | copy-start | bytes 3760132
Sparse Core Ops, SparseCore 0:
  140.5 93.8 all-gather.2
  259.7 165.4 all-reduce.6
  428.5 127.9 all-reduce.4
